TPU v7x, 32 devices: a whole 2x2x4 slice. The times are simulated.
32 devices in a mesh: groups: 2 (over x), row: 8 (over z, y), col: 2 (over core).
Axes of the slice: x: 2, y: 2, z: 4, core: 2. Of those that a mesh axis runs over, the one named last changes fastest.
Arguments:
- right_side: float32 [32, 4096], P('groups', ('row', 'col')), parts along dimension 0, may hold values from -6 to 6
- current_ratio: float32 [8192], P(('groups', 'row', 'col')), parts along dimension 0, may hold values from 0.7 to 1
- filament_xy: float32 [2, 6400], replicated, may hold values from -0.3 to 0.3
- element_offset: float32 [2, 8192], P(None, 'groups'), parts along dimension 1, may hold values from -0.003 to 0.003
- element_filament: int32 [8192], P('groups'), parts along dimension 0, may hold values from 0 to 6399
- element_order: int32 [8192], P('groups'), parts along dimension 0, may hold values from 0 to 4095, each once
Outputs:
- solution: float32 [32, 4096], P('groups', ('row', 'col')), parts along dimension 0
- residual: float32 [32, 4096], P('groups', ('row', 'col')), parts along dimension 0
There are 2 independent parts, one for each index of `groups`. A program takes and returns all parts, laid end to end along the dimension named above; an argument that names none is the same for every part. Nothing has to cross between parts.
Inputs may be any that keep to these rules, and one draw needn't show every extreme that they name: `element_order`: each position appears once.
All inputs are finite; a program needn't handle non-finite values.
Results may differ from a plain program's by a relative error of at most 0.00014.
Values sent between devices are 32-bit elements; how exact they have to be, the bound alone decides.
A program may use at most 128 MiB of HBM per device.

v0:
```python
import math

import jax
import jax.numpy as jnp
from jax import lax
from jax.sharding import PartitionSpec as P

ITERS = 2


EPS_SQUARED = 0.0001
COUPLE = 0.3


def kernel(left_x, left_y, right_x, right_y):
    delta_x = left_x[:, None] - right_x[None, :]
    delta_y = left_y[:, None] - right_y[None, :]
    return lax.rsqrt(delta_x * delta_x + delta_y * delta_y + EPS_SQUARED)


def on_device(
    right_side, current_ratio, filament_xy, element_offset, element_filament, element_order
):
    row_devices = lax.axis_size("row")
    col_devices = lax.axis_size("col")
    side_count = right_side.shape[0]
    local_count = right_side.shape[1]
    element_count = local_count * row_devices * col_devices
    coupling_scale = COUPLE / math.sqrt(element_count)
    places = filament_xy[:, element_filament[element_order]] + element_offset[:, element_order]
    diagonal = 1.0 + 8.0 * current_ratio**24
    row_index = lax.axis_index("row")
    col_index = lax.axis_index("col")
    col_width = local_count * col_devices
    col_xy = lax.dynamic_slice_in_dim(places, row_index * col_width, col_width, 1)
    row_xy = lax.dynamic_index_in_dim(
        places.reshape(2, row_devices, col_devices, local_count), col_index, 2, False
    )
    solution = jnp.zeros_like(right_side)
    residual = right_side
    direction = right_side

    def squares(vector):
        return lax.psum(jnp.sum(vector * vector, axis=1, keepdims=True), ("row", "col"))

    norm_now = squares(residual)
    for iteration in range(ITERS):
        wide = lax.all_gather(direction, "col", axis=1, tiled=True)
        peer_count = side_count * lax.axis_size("row") // side_count
        group_size = math.gcd(peer_count, 8)
        blocks = peer_count // group_size
        block_places = row_xy.reshape(2, blocks, group_size * local_count).transpose(1, 0, 2)

        def apply_block(block_xy):
            coupling = kernel(col_xy[0], col_xy[1], block_xy[0], block_xy[1])
            return jnp.dot(
                wide, coupling, precision=lax.Precision.HIGHEST, preferred_element_type=jnp.float32
            )

        parts = lax.map(apply_block, block_places)
        parts = parts.reshape(blocks, side_count, group_size, local_count).transpose(0, 2, 1, 3)
        summed = lax.psum_scatter(
            parts.reshape(peer_count * side_count, local_count),
            "row",
            scatter_dimension=0,
            tiled=True,
        )
        image_vec = diagonal * direction + coupling_scale * summed
        curved = lax.psum(jnp.sum(direction * image_vec, axis=1, keepdims=True), ("row", "col"))
        step_length = norm_now / curved
        solution = solution + step_length * direction
        residual = residual - step_length * image_vec
        norm_next = squares(residual)
        direction = residual + norm_next / norm_now * direction
        norm_now = norm_next
    return (solution, residual)


def solution(mesh):
    return jax.shard_map(
        on_device,
        mesh=mesh,
        in_specs=(
            P("groups", ("row", "col")),
            P(("groups", "row", "col")),
            P(),
            P(None, "groups"),
            P("groups"),
            P("groups"),
        ),
        out_specs=(P("groups", ("row", "col")), P("groups", ("row", "col"))),
        check_vma=False,
    )
```

profile of v0, /device:TPU:0, one launch (start us, length us, event | category | flops | bytes accessed | tf_op | source)
XLA Modules:
  0.0 302.2 jit_solution(8599823185604984722)
XLA Ops:
  7.2 0.7 fusion.12
  8.0 23.0 %gather_fusion = s32[4096]{0:T(1024)S(1)} fusion(s32[4096]{0:T(1024)S(1)} %copy-done, s32[4096]{0:T(1024)S(1)} %fusion.12), kind=kCustom, calls=%fused_computation | custom fusion | bytes 49152 | tf_op jit(solution)/shard_map/gather | solution.py:30
  31.1 1.1 copy.12
  32.2 2.0 copy.13
  34.1 15.7 %gather_fusion.2 = f32[4096,2]{1,0:T(8,128)} fusion(f32[2,4096]{0,1:T(8,128)} %copy.13, s32[4096]{0:T(1024)S(1)} %fusion.12), kind=kCustom, calls=%fused_computation.2 | custom fusion | bytes 81920 | tf_op jit(solution)/shard_map/gather | solution.py:30
  49.8 14.1 %gather_fusion.1 = f32[4096,2]{1,0:T(8,128)} fusion(f32[2,6400]{0,1:T(8,128)S(1)} %copy.12, s32[4096]{0:T(1024)S(1)} %broadcast_clamp_fusion), kind=kCustom, calls=%fused_computation.1 | custom fusion | bytes 81920 | tf_op jit(solution)/shard_map/gather | solution.py:30
  63.9 2.4 add.92
  66.7 0.9 dynamic-slice_reduce_fusion.1
  67.6 1.9 all_gather.6
  69.6 3.2 %fusion.1 = f32[2048,16]{0,1:T(8,128)S(1)} fusion(f32[16,512]{1,0:T(8,128)S(1)} %all_gather.6, f32[2048]{0:T(1024)S(1)} %bitcast.53, f32[512]{0:T(512)S(1)} %get-tuple-element.30, f32[2048]{0:T(1024)S(1)} %bitcast.51, f32[512]{0:T(512)S(1)} %get-tuple-element.24), kind=kOutput, calls=%fused_computation.5 | convolution fusion | flops 207618048 | bytes 184320 | tf_op jit(solution)/shard_map/while/body/eval_jaxpr/dot_general | solution.py:56
  72.9 0.7 copy.15
  73.7 63.9 %reduce-scatter.3.cloned.1.call-done = f32[16,256]{1,0:T(8,128)} async-done(((f32[128,256]{1,0:T(8,128)}), f32[16,256]{1,0:T(8,128)}) %reduce-scatter.3.cloned.1.call-update) | async-done | bytes 16400 | tf_op jit(solution)/shard_map/reduce_scatter | solution.py:62
  137.6 0.8 multiply_reduce_fusion.2
  138.4 29.7 %all-reduce = (f32[16,1]{0,1:T(1,128)S(1)}, f32[16,1]{0,1:T(1,128)S(1)}) all-reduce(f32[16,1]{0,1:T(1,128)S(1)} %bitcast.56, f32[16,1]{0,1:T(1,128)S(1)} %bitcast.55), channel_id=1, replica_groups=mesh['groups'=2,'row'=8,'col'=2] {'row','col'}, use_global_device_ids=true, to_apply=%region_1.2 | all-reduce | flops 32 | bytes 256 | tf_op jit(solution)/shard_map/psum | solution.py:44
  168.1 0.9 multiply_reduce_fusion.1
  169.0 29.5 %psum.30 = f32[16,1]{0,1:T(1,128)S(1)} all-reduce(f32[16,1]{0,1:T(1,128)S(1)} %bitcast.57), channel_id=1, replica_groups=mesh['groups'=2,'row'=8,'col'=2] {'row','col'}, use_global_device_ids=true, to_apply=%region_6.7 | all-reduce | flops 16 | bytes 128 | tf_op jit(solution)/shard_map/psum | solution.py:44
  198.5 0.8 multiply_add_fusion.2
  199.3 1.8 all_gather.7
  201.1 3.1 %fusion = f32[16,2048]{1,0:T(8,128)S(1)} fusion(f32[16,512]{1,0:T(8,128)S(1)} %all_gather.7, f32[2048]{0:T(1024)S(1)} %bitcast.54, f32[512]{0:T(512)S(1)} %get-tuple-element.30, f32[2048]{0:T(1024)S(1)} %bitcast.52, f32[512]{0:T(512)S(1)} %get-tuple-element.24), kind=kOutput, calls=%fused_computation.4 | convolution fusion | flops 207618048 | bytes 184320 | tf_op jit(solution)/shard_map/while/body/eval_jaxpr/dot_general | solution.py:56
  204.2 0.7 copy.16
  204.9 58.5 %reduce-scatter.5.cloned.1.call-done = f32[16,256]{1,0:T(8,128)} async-done(((f32[128,256]{1,0:T(8,128)}), f32[16,256]{1,0:T(8,128)}) %reduce-scatter.5.cloned.1.call-update) | async-done | bytes 16400 | tf_op jit(solution)/shard_map/reduce_scatter | solution.py:62
  263.4 0.8 multiply_reduce_fusion
  264.3 29.6 %psum.31 = f32[16,1]{0,1:T(1,128)S(1)} all-reduce(f32[16,1]{0,1:T(1,128)S(1)} %bitcast.58), channel_id=1, replica_groups=mesh['groups'=2,'row'=8,'col'=2] {'row','col'}, use_global_device_ids=true, to_apply=%region_9.10 | all-reduce | flops 16 | bytes 128 | tf_op jit(solution)/shard_map/psum | solution.py:69
  293.9 1.4 multiply_subtract_fusion
  (30 shorter events, 0.7 us)
Async XLA Ops:
  7.2 0.8 copy-start
  7.2 130.4 %reduce-scatter.3.cloned.1.call-start = ((), (), s32[]{:S(2)}) async-start(), calls=%async_computation.2 | async-start | bytes 147456 | tf_op jit(solution)/shard_map/reduce_scatter | solution.py:62
  8.0 23.1 %copy-start.3 = (f32[2,6400]{1,0:T(2,128)S(1)}, f32[2,6400]{1,0:T(2,128)}, u32[]{:S(2)}) copy-start(f32[2,6400]{1,0:T(2,128)} %param.8) | copy-start | bytes 153604
  31.0 1.2 copy-start.4
  63.9 3.7 %copy-start.1 = (f32[16,256]{1,0:T(8,128)S(1)}, f32[16,256]{1,0:T(8,128)}, u32[]{:S(2)}) copy-start(f32[16,256]{1,0:T(8,128)} %param.6) | copy-start | bytes 49156
  69.6 4.1 %copy-start.5 = (f32[256]{0:T(256)S(1)}, f32[256]{0:T(256)}, u32[]{:S(2)}) copy-start(f32[256]{0:T(256)} %param.7) | copy-start | bytes 3076
  73.6 189.9 %reduce-scatter.5.cloned.1.call-start = ((), (), s32[]{:S(2)}) async-start(), calls=%async_computation.3 | async-start | bytes 147456 | tf_op jit(solution)/shard_map/reduce_scatter | solution.py:62
  201.1 92.9 %copy-start.2 = (f32[16,256]{1,0:T(8,128)S(1)}, f32[16,256]{1,0:T(8,128)}, u32[]{:S(2)}) copy-start(f32[16,256]{1,0:T(8,128)} %reduce-scatter.3.cloned.1.call-done) | copy-start | bytes 49156
Sparse Core Ops, SparseCore 0:
  73.7 63.8 reduce-scatter.2
  205.0 58.3 reduce-scatter.4
where the time goes:
time: 303 us; the launch traced here: 302 us
  waiting for transfers between devices  122 us (40%)
  blocking collectives  92.5 us (31%)
  local copies, waits for them, and re-layouts  58.6 us (19%)
  between operations  14.2 us (5%)
  other arithmetic  8 us (3%)
  matrix products  6.3 us (2%)
    reduce_scatter x2, waiting for transfers between devices, on_device(): lax.psum_scatter(parts.reshape(peer_count * side_count, local_count), 'ro...  122 us
    psum x2, blocking collectives, squares(): lax.psum(jnp.sum(vector * vector, axis=1, keepdims=True), ('row', 'col'))  59.1 us
    psum x1, blocking collectives, on_device(): lax.psum(jnp.sum(direction * image_vec, axis=1, keepdims=True), ('row', '...  29.6 us
    gather x1, local copies, waits for them, and re-layouts, on_device(): element_filament[element_order]  23 us
    gather x1, local copies, waits for them, and re-layouts, on_device(): element_offset[:, element_order]  15.7 us
    gather x1, local copies, waits for them, and re-layouts, on_device(): filament_xy[:, element_filament[element_order]]  14.1 us
    dot_general x2, matrix products, apply_block(): jnp.dot(wide, coupling, precision=lax.Precision.HIGHEST, preferred_elemen...  6.3 us
  transfers between devices with their start and end apart: 2, of which 2 were waited for; matrix products, arithmetic and copies ran while one was open for 0% of the time, Pallas kernels for 0%

commit v1 on v0

v1 whole, which is shorter than its diff:
```python
import functools
import math

import jax
import jax.numpy as jnp
from jax import lax
from jax.experimental import pallas as pl
from jax.experimental.pallas import tpu as pltpu
from jax.sharding import PartitionSpec as P

EPS_SQUARED = 0.0001
COUPLE = 0.3
LANES = 128
MESH = pl.DeviceIdType.MESH


def loop(count, body):
    if count <= 16:
        for k in range(count):
            body(k)
    else:
        lax.fori_loop(0, count, lambda k, _: (body(k), 0)[1], 0)


def pick(table, index):
    rows, n = table.shape[0], index.shape[1]
    hot = (lax.broadcasted_iota(jnp.int32, (rows, n), 0) == (index >> 7)).astype(jnp.float32)
    taken = lax.dot_general(
        table.T, hot, (((1,), (0,)), ((), ())), precision=lax.Precision.HIGHEST, preferred_element_type=jnp.float32
    )
    lane = lax.broadcasted_iota(jnp.int32, (LANES, n), 0)
    return jnp.sum(jnp.where(lane == (index & (LANES - 1)), taken, 0.0), axis=0, keepdims=True)


def split(value):
    high = value.astype(jnp.bfloat16)
    low = (value - high.astype(jnp.float32)).astype(jnp.bfloat16)
    return high, low


def kernel(
    rows, cols, scale,
    b_ref, ratio_ref, xy_ref, offset_ref, filament_ref, order_ref,
    solution_ref, residual_ref,
    offset_tab, xy_tab, near, b_all, xy_all, image_all, r_all, dots,
    send_b, recv_b, send_xy, recv_xy, send_im, recv_im, send_dot, recv_dot,
):
    count = rows * cols
    side, width = b_ref.shape
    group = lax.axis_index("groups")
    me = lax.axis_index("row") * cols + lax.axis_index("col")

    def peer(off):
        return lax.rem(me + off, count)

    def device(p):
        return (group, p // cols, lax.rem(p, cols))

    def copy(src, dst_all, send, recv, off):
        return pltpu.make_async_remote_copy(
            src_ref=src, dst_ref=dst_all.at[me], send_sem=send.at[off - 1], recv_sem=recv.at[me],
            device_id=device(peer(off)), device_id_type=MESH,
        )

    def arrived(dst_all, send, recv, p):
        pltpu.make_async_remote_copy(
            src_ref=dst_all.at[p], dst_ref=dst_all.at[p], send_sem=send.at[0], recv_sem=recv.at[p],
            device_id=device(peer(1)), device_id_type=MESH,
        ).wait_recv()

    barrier = pltpu.get_barrier_semaphore()
    loop(count - 1, lambda k: pl.semaphore_signal(barrier, inc=1, device_id=device(peer(k + 1)), device_id_type=MESH))

    for ref, tab in ((offset_ref, offset_tab), (xy_ref, xy_tab)):
        for axis in range(2):
            for q in range(ref.shape[1] // LANES):
                tab[axis, q : q + 1, :] = ref[axis : axis + 1, q * LANES : (q + 1) * LANES]
    parts = width // LANES
    order = jnp.concatenate([order_ref[pl.ds(me * parts + k, 1), :] for k in range(parts)], axis=1)
    filament = (pick(filament_ref[...].astype(jnp.float32), order) + 0.5).astype(jnp.int32)
    for axis in range(2):
        place = pick(xy_tab[axis], filament) + pick(offset_tab[axis], order)
        xy_all[me, axis : axis + 1, :] = place
        near[axis] = jnp.broadcast_to(place, (width, width)).T
    b_all[me] = b_ref[...]

    pl.semaphore_wait(barrier, count - 1)
    loop(count - 1, lambda k: copy(xy_all.at[me], xy_all, send_xy, recv_xy, k + 1).start())
    loop(count - 1, lambda k: copy(b_ref, b_all, send_b, recv_b, k + 1).start())

    ratio = ratio_ref[...]
    cube = ratio * ratio * ratio
    sixth = cube * cube
    twelfth = sixth * sixth
    diagonal = 1.0 + 8.0 * (twelfth * twelfth)

    def term(p, vector, total):
        dx = near[0] - xy_all[p, 0:1, :]
        dy = near[1] - xy_all[p, 1:2, :]
        coupling = lax.rsqrt(dx * dx + dy * dy + EPS_SQUARED)
        c_high, c_low = split(coupling)
        v_high, v_low = split(vector)
        contract = (((1,), (1,)), ((), ()))
        both = lax.dot_general(
            jnp.concatenate([v_high, v_low], axis=0), c_high, contract, preferred_element_type=jnp.float32
        )
        rest = lax.dot_general(v_high, c_low, contract, preferred_element_type=jnp.float32)
        return total + both[:side] + (both[side:] + rest)

    zero = jnp.zeros((side, width), jnp.float32)

    def rowsum(value):
        return jnp.sum(value, axis=1, keepdims=True)

    b = b_ref[...]
    total = term(me, b, zero)

    def first(k, carry):
        total, squares = carry
        p = peer(k)
        arrived(xy_all, send_xy, recv_xy, p)
        arrived(b_all, send_b, recv_b, p)
        value = b_all[p]
        return term(p, value, total), squares + value * value

    total, squares = lax.fori_loop(1, count, first, (total, b * b))
    image = diagonal * b + scale * total
    image_all[me] = image
    loop(count - 1, lambda k: copy(image_all.at[me], image_all, send_im, recv_im, k + 1).start())
    norm = rowsum(squares)

    def curve(k, carry):
        p = peer(k)
        arrived(image_all, send_im, recv_im, p)
        return carry + b_all[p] * image_all[p]

    curved = rowsum(lax.fori_loop(1, count, curve, b * image))
    step = norm / curved

    def reduce_residual(k, carry):
        value = b_all[k] - step * image_all[k]
        r_all[k] = value
        return carry + value * value

    norm_next = rowsum(lax.fori_loop(0, count, reduce_residual, zero))
    beta = norm_next / norm

    def second(k, total):
        return term(k, r_all[k] + beta * b_all[k], total)

    total = lax.fori_loop(0, count, second, zero)
    residual = r_all[me]
    direction = residual + beta * b
    image2 = diagonal * direction + scale * total

    own = (
        lax.broadcasted_iota(jnp.int32, (side, LANES), 0) == lax.broadcasted_iota(jnp.int32, (side, LANES), 1)
    )
    partial = rowsum(direction * image2)
    dots[me] = jnp.sum(jnp.where(own, partial, 0.0), axis=0, keepdims=True)
    loop(count - 1, lambda k: copy(dots.at[me], dots, send_dot, recv_dot, k + 1).start())
    loop(count - 1, lambda k: arrived(dots, send_dot, recv_dot, peer(k + 1)))
    row = lax.fori_loop(0, count, lambda k, acc: acc + dots[k], jnp.zeros((1, LANES), jnp.float32))
    curved2 = rowsum(jnp.where(own, row, 0.0))
    step2 = norm_next / curved2
    solution_ref[...] = step * b + step2 * direction
    residual_ref[...] = residual - step2 * image2

    for src, dst, send, recv in (
        (b_ref, b_all, send_b, recv_b),
        (xy_all.at[me], xy_all, send_xy, recv_xy),
        (image_all.at[me], image_all, send_im, recv_im),
        (dots.at[me], dots, send_dot, recv_dot),
    ):
        loop(count - 1, lambda k: copy(src, dst, send, recv, k + 1).wait_send())


def solution(mesh):
    rows, cols = mesh.shape["row"], mesh.shape["col"]
    count = rows * cols

    def on_device(right_side, current_ratio, filament_xy, element_offset, element_filament, element_order):
        side, width = right_side.shape
        elements = width * count
        shape = jax.ShapeDtypeStruct((side, width), jnp.float32)
        vmem = pl.BlockSpec(memory_space=pltpu.VMEM)
        f32 = jnp.float32
        blocks = pltpu.VMEM((count, side, width), f32)
        return pl.pallas_call(
            functools.partial(kernel, rows, cols, COUPLE / math.sqrt(elements)),
            out_shape=(shape, shape),
            in_specs=[vmem] * 6,
            out_specs=(vmem, vmem),
            scratch_shapes=[
                pltpu.VMEM((2, elements // LANES, LANES), f32),
                pltpu.VMEM((2, filament_xy.shape[1] // LANES, LANES), f32),
                pltpu.VMEM((2, width, width), f32),
                blocks,
                pltpu.VMEM((count, 2, width), f32),
                blocks,
                blocks,
                pltpu.VMEM((count, 1, LANES), f32),
            ]
            + [pltpu.SemaphoreType.DMA((count,))] * 8,
            compiler_params=pltpu.CompilerParams(
                collective_id=0, has_side_effects=True, vmem_limit_bytes=24 * 1024 * 1024
            ),
        )(
            right_side,
            current_ratio.reshape(1, width),
            filament_xy,
            element_offset,
            element_filament.reshape(elements // LANES, LANES),
            element_order.reshape(elements // LANES, LANES),
        )

    return jax.shard_map(
        on_device,
        mesh=mesh,
        in_specs=(
            P("groups", ("row", "col")),
            P(("groups", "row", "col")),
            P(),
            P(None, "groups"),
            P("groups"),
            P("groups"),
        ),
        out_specs=(P("groups", ("row", "col")), P("groups", ("row", "col"))),
        check_vma=False,
    )
```

time: 303 us -> 40.6 us (0.13)
  waiting for transfers between devices: 122 us -> 0 us
  blocking collectives: 92.5 us -> 0 us
  local copies, waits for them, and re-layouts: 58.6 us -> 5.6 us
  Pallas kernels: 0 us -> 33.9 us
  between operations: 14.2 us -> 0.65 us
  other arithmetic: 8 us -> 0 us
  matrix products: 6.3 us -> 0 us
    reduce_scatter x2 -> x0, waiting for transfers between devices: 122 us -> none  [on_device(): lax.psum_scatter(parts.reshape(peer_count * side_count, local_count), 'ro...]
    psum x3 -> x0, blocking collectives: 88.8 us -> none  [the longest x2 59.1 us: squares(): lax.psum(jnp.sum(vector * vector, axis=1, keepdims=True), ('row', 'col'))]
    gather x3 -> x0, local copies, waits for them, and re-layouts: 52.8 us -> none  [the longest x1 23 us: on_device(): element_filament[element_order]]
    pallas_call x0 -> x1, Pallas kernels: none -> 33.9 us  [on_device(): pl.pallas_call(functools.partial(kernel, rows, cols, COUPLE / math.sqrt(e...]
    dot_general x2 -> x0, matrix products: 6.3 us -> none  [apply_block(): jnp.dot(wide, coupling, precision=lax.Precision.HIGHEST, preferred_elemen...]
    all_gather x2 -> x0, blocking collectives: 3.76 us -> none  [on_device(): wide = lax.all_gather(direction, 'col', axis=1, tiled=True)]
    add x3 -> x0, other arithmetic: 3.25 us -> none  [the longest x1 2.45 us: on_device(): filament_xy[:, element_filament[element_order]]]
  transfers between devices with their start and end apart: 2 -> 0, of which waited for: 2 -> 0; matrix products, arithmetic and copies ran while one was open for 0% -> 0% of each run, Pallas kernels for 0% -> 0%
where the time goes in v1:
time: 40.6 us; the launch traced here: 40.2 us
  Pallas kernels  33.9 us (83%)
  local copies, waits for them, and re-layouts  5.6 us (14%)
  between operations  0.65 us (2%)
    pallas_call x1, Pallas kernels, on_device(): pl.pallas_call(functools.partial(kernel, rows, cols, COUPLE / math.sqrt(e...  33.9 us
    unnamed x14, local copies, waits for them, and re-layouts  5.6 us

profile of v1, /device:TPU:0, one launch (start us, length us, event | category | flops | bytes accessed | tf_op | source)
XLA Modules:
  0.0 40.2 jit_solution(5726904772311276186)
XLA Ops:
  0.6 0.0 copy-start.5
  0.6 0.7 %copy-done.5 = f32[256]{0:T(256)S(1)} copy-done((f32[256]{0:T(256)S(1)}, f32[256]{0:T(256)}, u32[]{:S(2)}) %copy-start.5) | copy-done | bytes 1048
  1.3 0.0 copy-start
  1.3 0.8 %copy-done = f32[2,6400]{1,0:T(2,128)S(1)} copy-done((f32[2,6400]{1,0:T(2,128)S(1)}, f32[2,6400]{1,0:T(2,128)}, u32[]{:S(2)}) %copy-start) | copy-done | bytes 51224
  2.1 0.0 copy-start.1
  2.1 0.8 %copy-done.1 = f32[2,4096]{1,0:T(2,128)S(1)} copy-done((f32[2,4096]{1,0:T(2,128)S(1)}, f32[2,4096]{1,0:T(2,128)}, u32[]{:S(2)}) %copy-start.1) | copy-done | bytes 32792
  2.9 0.0 copy-start.2
  2.9 0.7 %copy-done.2 = f32[16,256]{1,0:T(8,128)S(1)} copy-done((f32[16,256]{1,0:T(8,128)S(1)}, f32[16,256]{1,0:T(8,128)}, u32[]{:S(2)}) %copy-start.2) | copy-done | bytes 16408
  3.6 0.0 copy-start.3
  3.6 0.7 %copy-done.3 = s32[4096]{0:T(1024)S(1)} copy-done((s32[4096]{0:T(1024)S(1)}, s32[4096]{0:T(1024)}, u32[]{:S(2)}) %copy-start.3) | copy-done | bytes 16408
  4.3 0.0 copy-start.4
  4.3 0.7 %copy-done.4 = s32[4096]{0:T(1024)S(1)} copy-done((s32[4096]{0:T(1024)S(1)}, s32[4096]{0:T(1024)}, u32[]{:S(2)}) %copy-start.4) | copy-done | bytes 16408
  5.0 33.9 %shard_map.77 = (f32[16,256]{1,0:T(8,128)S(1)}, f32[16,256]{1,0:T(8,128)S(1)}) custom-call(f32[16,256]{1,0:T(8,128)S(1)} %copy-done.2, f32[1,256]{1,0:T(1,128)S(1)} %bitcast.5, f32[2,6400]{1,0:T(2,128)S(1)} %copy-done, f32[2,4096]{1,0:T(2,128)S(1)} %copy-done.1, s32[32,128]{1,0:T(8,128)S(1)} %bitcast.3, s32[32,128]{1,0:T(8,128)S(1)} %bitcast.4), custom_call_target="tpu_custom_call" | custom-call | tf_op jit(solution)/shard_map/pallas_call | solution.py:189
  39.0 0.6 %copy.10 = f32[16,256]{1,0:T(8,128)} copy(f32[16,256]{1,0:T(8,128)S(1)} %get-tuple-element.4) | data formatting | bytes 32768
  39.6 0.6 %copy.11 = f32[16,256]{1,0:T(8,128)} copy(f32[16,256]{1,0:T(8,128)S(1)} %get-tuple-element.5) | data formatting | bytes 32768
Async XLA Ops:
  0.6 0.7 %copy-start.5 = (f32[256]{0:T(256)S(1)}, f32[256]{0:T(256)}, u32[]{:S(2)}) copy-start(f32[256]{0:T(256)} %param.7) | copy-start | bytes 3076
  1.3 0.8 %copy-start = (f32[2,6400]{1,0:T(2,128)S(1)}, f32[2,6400]{1,0:T(2,128)}, u32[]{:S(2)}) copy-start(f32[2,6400]{1,0:T(2,128)} %xy_ref.1) | copy-start | bytes 153604
  2.1 0.8 %copy-start.1 = (f32[2,4096]{1,0:T(2,128)S(1)}, f32[2,4096]{1,0:T(2,128)}, u32[]{:S(2)}) copy-start(f32[2,4096]{1,0:T(2,128)} %offset_ref.1) | copy-start | bytes 98308
  2.9 0.7 %copy-start.2 = (f32[16,256]{1,0:T(8,128)S(1)}, f32[16,256]{1,0:T(8,128)}, u32[]{:S(2)}) copy-start(f32[16,256]{1,0:T(8,128)} %b_ref.1) | copy-start | bytes 49156
  3.6 0.7 %copy-start.3 = (s32[4096]{0:T(1024)S(1)}, s32[4096]{0:T(1024)}, u32[]{:S(2)}) copy-start(s32[4096]{0:T(1024)} %param.10) | copy-start | bytes 49156
  4.3 0.7 %copy-start.4 = (s32[4096]{0:T(1024)S(1)}, s32[4096]{0:T(1024)}, u32[]{:S(2)}) copy-start(s32[4096]{0:T(1024)} %param.11) | copy-start | bytes 49156

commit v2 on v1

--- a/solution.py
+++ b/solution.py
@@ -40,37 +40,77 @@
 
 def kernel(
     rows, cols, scale,
+    b_hbm, ratio_hbm, xy_hbm, offset_hbm, filament_hbm, order_hbm,
+    solution_ref, residual_ref,
     b_ref, ratio_ref, xy_ref, offset_ref, filament_ref, order_ref,
-    solution_ref, residual_ref,
     offset_tab, xy_tab, near, b_all, xy_all, image_all, r_all, dots,
-    send_b, recv_b, send_xy, recv_xy, send_im, recv_im, send_dot, recv_dot,
+    load, send_b, recv_b, send_xy, recv_xy, send_im, recv_im, send_dot, recv_dot,
 ):
     count = rows * cols
     side, width = b_ref.shape
     group = lax.axis_index("groups")
-    me = lax.axis_index("row") * cols + lax.axis_index("col")
-
-    def peer(off):
-        return lax.rem(me + off, count)
+    row, col = lax.axis_index("row"), lax.axis_index("col")
+    me = row * cols + col
+
+    loads = [
+        pltpu.make_async_copy(src, dst, load.at[k])
+        for k, (src, dst) in enumerate(
+            (
+                (order_hbm, order_ref), (filament_hbm, filament_ref), (offset_hbm, offset_ref),
+                (xy_hbm, xy_ref), (b_hbm, b_ref), (ratio_hbm, ratio_ref),
+            )
+        )
+    ]
+    for one in loads:
+        one.start()
+
+    def row_at(k):
+        return lax.rem(row + k, rows)
+
+    def col_at(c):
+        return lax.rem(col + c, cols)
 
     def device(p):
         return (group, p // cols, lax.rem(p, cols))
 
-    def copy(src, dst_all, send, recv, off):
+    def peer(k):
+        return lax.rem(me + k, count)
+
+    def push(src, dst, send, recv, device_id):
         return pltpu.make_async_remote_copy(
-            src_ref=src, dst_ref=dst_all.at[me], send_sem=send.at[off - 1], recv_sem=recv.at[me],
-            device_id=device(peer(off)), device_id_type=MESH,
-        )
-
-    def arrived(dst_all, send, recv, p):
-        pltpu.make_async_remote_copy(
-            src_ref=dst_all.at[p], dst_ref=dst_all.at[p], send_sem=send.at[0], recv_sem=recv.at[p],
-            device_id=device(peer(1)), device_id_type=MESH,
-        ).wait_recv()
+            src_ref=src, dst_ref=dst, send_sem=send, recv_sem=recv, device_id=device_id, device_id_type=MESH
+        )
+
+    def across(src, dst_all, send, recv, k):
+        return push(src, dst_all.at[me], send.at[k], recv.at[me], (group, row_at(k), col))
+
+    def beside(src, dst_all, send, recv, k, c):
+        p = row_at(k) * cols + col
+        src = dst_all.at[p] if src is None else src
+        return push(src, dst_all.at[p], send.at[rows + k * cols + c], recv.at[p], (group, row, col_at(c)))
+
+    def spread(src, dst_all, send, recv):
+        loop(rows - 1, lambda k: across(src, dst_all, send, recv, k + 1).start())
+        loop(cols - 1, lambda c: beside(src, dst_all, send, recv, 0, c + 1).start())
+
+    def forward(dst_all, send, recv, k):
+        arrived(dst_all, recv, row_at(k) * cols + col)
+        for c in range(1, cols):
+            beside(None, dst_all, send, recv, k, c).start()
+
+    def arrived(dst_all, recv, p):
+        push(dst_all.at[p], dst_all.at[p], send_b.at[0], recv.at[p], device(peer(1))).wait_recv()
+
+    def sent(src, dst_all, send, recv):
+        loop(rows - 1, lambda k: across(src, dst_all, send, recv, k + 1).wait_send())
+        for c in range(1, cols):
+            loop(rows, lambda k: beside(None, dst_all, send, recv, k, c).wait_send())
 
     barrier = pltpu.get_barrier_semaphore()
     loop(count - 1, lambda k: pl.semaphore_signal(barrier, inc=1, device_id=device(peer(k + 1)), device_id_type=MESH))
 
+    for one in loads:
+        one.wait()
     for ref, tab in ((offset_ref, offset_tab), (xy_ref, xy_tab)):
         for axis in range(2):
             for q in range(ref.shape[1] // LANES):
@@ -78,16 +118,17 @@
     parts = width // LANES
     order = jnp.concatenate([order_ref[pl.ds(me * parts + k, 1), :] for k in range(parts)], axis=1)
     filament = (pick(filament_ref[...].astype(jnp.float32), order) + 0.5).astype(jnp.int32)
+    places = [pick(xy_tab[axis], filament) + pick(offset_tab[axis], order) for axis in range(2)]
     for axis in range(2):
-        place = pick(xy_tab[axis], filament) + pick(offset_tab[axis], order)
-        xy_all[me, axis : axis + 1, :] = place
-        near[axis] = jnp.broadcast_to(place, (width, width)).T
+        xy_all[me, axis : axis + 1, :] = places[axis]
     b_all[me] = b_ref[...]
 
     pl.semaphore_wait(barrier, count - 1)
-    loop(count - 1, lambda k: copy(xy_all.at[me], xy_all, send_xy, recv_xy, k + 1).start())
-    loop(count - 1, lambda k: copy(b_ref, b_all, send_b, recv_b, k + 1).start())
-
+    spread(xy_all.at[me], xy_all, send_xy, recv_xy)
+    spread(b_ref, b_all, send_b, recv_b)
+
+    for axis in range(2):
+        near[axis] = jnp.broadcast_to(places[axis], (width, width)).T
     ratio = ratio_ref[...]
     cube = ratio * ratio * ratio
     sixth = cube * cube
@@ -112,29 +153,49 @@
     def rowsum(value):
         return jnp.sum(value, axis=1, keepdims=True)
 
+    def other(k):
+        return row_at(k // (cols - 1)) * cols + col_at(1 + lax.rem(k, cols - 1))
+
+    others = rows * (cols - 1)
+
     b = b_ref[...]
     total = term(me, b, zero)
 
-    def first(k, carry):
+    def add_first(p, carry):
         total, squares = carry
-        p = peer(k)
-        arrived(xy_all, send_xy, recv_xy, p)
-        arrived(b_all, send_b, recv_b, p)
         value = b_all[p]
         return term(p, value, total), squares + value * value
 
-    total, squares = lax.fori_loop(1, count, first, (total, b * b))
+    def first(k, carry):
+        forward(xy_all, send_xy, recv_xy, k)
+        forward(b_all, send_b, recv_b, k)
+        return add_first(row_at(k) * cols + col, carry)
+
+    def first_other(k, carry):
+        p = other(k)
+        arrived(xy_all, recv_xy, p)
+        arrived(b_all, recv_b, p)
+        return add_first(p, carry)
+
+    carry = lax.fori_loop(1, rows, first, (total, b * b))
+    total, squares = lax.fori_loop(0, others, first_other, carry)
     image = diagonal * b + scale * total
     image_all[me] = image
-    loop(count - 1, lambda k: copy(image_all.at[me], image_all, send_im, recv_im, k + 1).start())
+    spread(image_all.at[me], image_all, send_im, recv_im)
     norm = rowsum(squares)
 
     def curve(k, carry):
-        p = peer(k)
-        arrived(image_all, send_im, recv_im, p)
+        forward(image_all, send_im, recv_im, k)
+        p = row_at(k) * cols + col
         return carry + b_all[p] * image_all[p]
 
-    curved = rowsum(lax.fori_loop(1, count, curve, b * image))
+    def curve_other(k, carry):
+        p = other(k)
+        arrived(image_all, recv_im, p)
+        return carry + b_all[p] * image_all[p]
+
+    carry = lax.fori_loop(1, rows, curve, b * image)
+    curved = rowsum(lax.fori_loop(0, others, curve_other, carry))
     step = norm / curved
 
     def reduce_residual(k, carry):
@@ -158,21 +219,22 @@
     )
     partial = rowsum(direction * image2)
     dots[me] = jnp.sum(jnp.where(own, partial, 0.0), axis=0, keepdims=True)
-    loop(count - 1, lambda k: copy(dots.at[me], dots, send_dot, recv_dot, k + 1).start())
-    loop(count - 1, lambda k: arrived(dots, send_dot, recv_dot, peer(k + 1)))
-    row = lax.fori_loop(0, count, lambda k, acc: acc + dots[k], jnp.zeros((1, LANES), jnp.float32))
-    curved2 = rowsum(jnp.where(own, row, 0.0))
+
+    def give(k):
+        return push(dots.at[me], dots.at[me], send_dot.at[k], recv_dot.at[me], device(peer(k)))
+
+    loop(count - 1, lambda k: give(k + 1).start())
+    loop(count - 1, lambda k: arrived(dots, recv_dot, peer(k + 1)))
+    flat = lax.fori_loop(0, count, lambda k, acc: acc + dots[k], jnp.zeros((1, LANES), jnp.float32))
+    curved2 = rowsum(jnp.where(own, flat, 0.0))
     step2 = norm_next / curved2
     solution_ref[...] = step * b + step2 * direction
     residual_ref[...] = residual - step2 * image2
 
-    for src, dst, send, recv in (
-        (b_ref, b_all, send_b, recv_b),
-        (xy_all.at[me], xy_all, send_xy, recv_xy),
-        (image_all.at[me], image_all, send_im, recv_im),
-        (dots.at[me], dots, send_dot, recv_dot),
-    ):
-        loop(count - 1, lambda k: copy(src, dst, send, recv, k + 1).wait_send())
+    sent(b_ref, b_all, send_b, recv_b)
+    sent(xy_all.at[me], xy_all, send_xy, recv_xy)
+    sent(image_all.at[me], image_all, send_im, recv_im)
+    loop(count - 1, lambda k: give(k + 1).wait_send())
 
 
 def solution(mesh):
@@ -189,9 +251,15 @@
         return pl.pallas_call(
             functools.partial(kernel, rows, cols, COUPLE / math.sqrt(elements)),
             out_shape=(shape, shape),
-            in_specs=[vmem] * 6,
+            in_specs=[pl.BlockSpec(memory_space=pltpu.HBM)] * 6,
             out_specs=(vmem, vmem),
             scratch_shapes=[
+                pltpu.VMEM((side, width), f32),
+                pltpu.VMEM((1, width), f32),
+                pltpu.VMEM(filament_xy.shape, f32),
+                pltpu.VMEM(element_offset.shape, f32),
+                pltpu.VMEM((elements // LANES, LANES), jnp.int32),
+                pltpu.VMEM((elements // LANES, LANES), jnp.int32),
                 pltpu.VMEM((2, elements // LANES, LANES), f32),
                 pltpu.VMEM((2, filament_xy.shape[1] // LANES, LANES), f32),
                 pltpu.VMEM((2, width, width), f32),
@@ -201,9 +269,10 @@
                 blocks,
                 pltpu.VMEM((count, 1, LANES), f32),
             ]
-            + [pltpu.SemaphoreType.DMA((count,))] * 8,
+            + [pltpu.SemaphoreType.DMA((6,))]
+            + [pltpu.SemaphoreType.DMA((rows * (1 + cols),)), pltpu.SemaphoreType.DMA((count,))] * 4,
             compiler_params=pltpu.CompilerParams(
-                collective_id=0, has_side_effects=True, vmem_limit_bytes=24 * 1024 * 1024
+                collective_id=0, has_side_effects=True, vmem_limit_bytes=60 * 1024 * 1024
             ),
         )(
             right_side,

time: 40.6 us -> 32.9 us (0.81)
  Pallas kernels: 33.9 us -> 30 us
  local copies, waits for them, and re-layouts: 5.6 us -> 1.94 us
    pallas_call x1, Pallas kernels: 33.9 us -> 30 us  [on_device(): pl.pallas_call(functools.partial(kernel, rows, cols, COUPLE / math.sqrt(e...]
    unnamed x14 -> x4, local copies, waits for them, and re-layouts: 5.6 us -> 1.94 us
where the time goes in v2:
time: 32.9 us; the launch traced here: 32.6 us
  Pallas kernels  30 us (91%)
  local copies, waits for them, and re-layouts  1.94 us (6%)
  between operations  0.65 us (2%)
    pallas_call x1, Pallas kernels, on_device(): pl.pallas_call(functools.partial(kernel, rows, cols, COUPLE / math.sqrt(e...  30 us
    unnamed x4, local copies, waits for them, and re-layouts  1.94 us

profile of v2, /device:TPU:0, one launch (start us, length us, event | category | flops | bytes accessed | tf_op | source)
XLA Modules:
  0.0 32.6 jit_solution(8836505293472525381)
XLA Ops:
  0.6 30.0 %shard_map.77 = (f32[16,256]{1,0:T(8,128)}, f32[16,256]{1,0:T(8,128)}) custom-call(f32[16,256]{1,0:T(8,128)} %b_hbm.1, f32[1,256]{1,0:T(1,128)} %bitcast.5, f32[2,6400]{1,0:T(2,128)} %xy_hbm.1, f32[2,4096]{1,0:T(2,128)} %offset_hbm.1, s32[32,128]{1,0:T(8,128)} %bitcast.3, s32[32,128]{1,0:T(8,128)} %bitcast.4), custom_call_target="tpu_custom_call" | custom-call | tf_op jit(solution)/shard_map/pallas_call | solution.py:251
  30.7 0.0 copy-start
  30.7 1.3 %copy.10 = f32[16,256]{1,0:T(8,128)} copy(f32[16,256]{1,0:T(8,128)} %get-tuple-element.4) | data formatting | bytes 32768
  32.0 0.0 copy-done
  32.0 0.6 %copy.11 = f32[16,256]{1,0:T(8,128)} copy(f32[16,256]{1,0:T(8,128)S(1)} %copy-done) | data formatting | bytes 32768
Async XLA Ops:
  30.7 1.3 %copy-start = (f32[16,256]{1,0:T(8,128)S(1)}, f32[16,256]{1,0:T(8,128)}, u32[]{:S(2)}) copy-start(f32[16,256]{1,0:T(8,128)} %get-tuple-element.5) | copy-start | bytes 49156

commit v3 on v2

--- a/solution.py
+++ b/solution.py
@@ -20,6 +20,14 @@
             body(k)
     else:
         lax.fori_loop(0, count, lambda k, _: (body(k), 0)[1], 0)
+
+
+def fold(start, stop, body, carry):
+    if stop - start <= 16:
+        for k in range(start, stop):
+            carry = body(k, carry)
+        return carry
+    return lax.fori_loop(start, stop, body, carry)
 
 
 def pick(table, index):
@@ -43,7 +51,7 @@
     b_hbm, ratio_hbm, xy_hbm, offset_hbm, filament_hbm, order_hbm,
     solution_ref, residual_ref,
     b_ref, ratio_ref, xy_ref, offset_ref, filament_ref, order_ref,
-    offset_tab, xy_tab, near, b_all, xy_all, image_all, r_all, dots,
+    offset_tab, xy_tab, near, high_all, low_all, b_all, xy_all, image_all, r_all, dots,
     load, send_b, recv_b, send_xy, recv_xy, send_im, recv_im, send_dot, recv_dot,
 ):
     count = rows * cols
@@ -123,10 +131,6 @@
         xy_all[me, axis : axis + 1, :] = places[axis]
     b_all[me] = b_ref[...]
 
-    pl.semaphore_wait(barrier, count - 1)
-    spread(xy_all.at[me], xy_all, send_xy, recv_xy)
-    spread(b_ref, b_all, send_b, recv_b)
-
     for axis in range(2):
         near[axis] = jnp.broadcast_to(places[axis], (width, width)).T
     ratio = ratio_ref[...]
@@ -135,18 +139,24 @@
     twelfth = sixth * sixth
     diagonal = 1.0 + 8.0 * (twelfth * twelfth)
 
-    def term(p, vector, total):
+    def couple(p):
         dx = near[0] - xy_all[p, 0:1, :]
         dy = near[1] - xy_all[p, 1:2, :]
-        coupling = lax.rsqrt(dx * dx + dy * dy + EPS_SQUARED)
-        c_high, c_low = split(coupling)
+        high_all[p], low_all[p] = split(lax.rsqrt(dx * dx + dy * dy + EPS_SQUARED))
+
+    def term(p, vector, total):
         v_high, v_low = split(vector)
         contract = (((1,), (1,)), ((), ()))
         both = lax.dot_general(
-            jnp.concatenate([v_high, v_low], axis=0), c_high, contract, preferred_element_type=jnp.float32
+            jnp.concatenate([v_high, v_low], axis=0), high_all[p], contract, preferred_element_type=jnp.float32
         )
-        rest = lax.dot_general(v_high, c_low, contract, preferred_element_type=jnp.float32)
+        rest = lax.dot_general(v_high, low_all[p], contract, preferred_element_type=jnp.float32)
         return total + both[:side] + (both[side:] + rest)
+
+    couple(me)
+    pl.semaphore_wait(barrier, count - 1)
+    spread(xy_all.at[me], xy_all, send_xy, recv_xy)
+    spread(b_ref, b_all, send_b, recv_b)
 
     zero = jnp.zeros((side, width), jnp.float32)
 
@@ -160,6 +170,21 @@
 
     b = b_ref[...]
     total = term(me, b, zero)
+
+    def gather_xy(k, carry):
+        forward(xy_all, send_xy, recv_xy, k)
+        couple(row_at(k) * cols + col)
+        return carry
+
+    def gather_b(k, carry):
+        forward(b_all, send_b, recv_b, k)
+        return carry
+
+    def couple_other(k, carry):
+        p = other(k)
+        arrived(xy_all, recv_xy, p)
+        couple(p)
+        return carry
 
     def add_first(p, carry):
         total, squares = carry
@@ -167,18 +192,19 @@
         return term(p, value, total), squares + value * value
 
     def first(k, carry):
-        forward(xy_all, send_xy, recv_xy, k)
-        forward(b_all, send_b, recv_b, k)
         return add_first(row_at(k) * cols + col, carry)
 
     def first_other(k, carry):
         p = other(k)
-        arrived(xy_all, recv_xy, p)
         arrived(b_all, recv_b, p)
         return add_first(p, carry)
 
-    carry = lax.fori_loop(1, rows, first, (total, b * b))
-    total, squares = lax.fori_loop(0, others, first_other, carry)
+    lax.fori_loop(1, rows, gather_xy, 0)
+    couple_other(0, 0)
+    lax.fori_loop(1, rows, lambda k, carry: couple_other(k, gather_b(k, carry)), 0)
+    lax.fori_loop(rows, others, couple_other, 0)
+    carry = fold(1, rows, first, (total, b * b))
+    total, squares = fold(0, others, first_other, carry)
     image = diagonal * b + scale * total
     image_all[me] = image
     spread(image_all.at[me], image_all, send_im, recv_im)
@@ -203,13 +229,13 @@
         r_all[k] = value
         return carry + value * value
 
-    norm_next = rowsum(lax.fori_loop(0, count, reduce_residual, zero))
+    norm_next = rowsum(fold(0, count, reduce_residual, zero))
     beta = norm_next / norm
 
     def second(k, total):
         return term(k, r_all[k] + beta * b_all[k], total)
 
-    total = lax.fori_loop(0, count, second, zero)
+    total = fold(0, count, second, zero)
     residual = r_all[me]
     direction = residual + beta * b
     image2 = diagonal * direction + scale * total
@@ -263,6 +289,8 @@
                 pltpu.VMEM((2, elements // LANES, LANES), f32),
                 pltpu.VMEM((2, filament_xy.shape[1] // LANES, LANES), f32),
                 pltpu.VMEM((2, width, width), f32),
+                pltpu.VMEM((count, width, width), jnp.bfloat16),
+                pltpu.VMEM((count, width, width), jnp.bfloat16),
                 blocks,
                 pltpu.VMEM((count, 2, width), f32),
                 blocks,

time: 32.9 us -> 30.9 us (0.939)
  Pallas kernels: 30 us -> 28.1 us
    pallas_call x1, Pallas kernels: 30 us -> 28.1 us  [on_device(): pl.pallas_call(functools.partial(kernel, rows, cols, COUPLE / math.sqrt(e...]
where the time goes in v3:
time: 30.9 us; the launch traced here: 30.7 us
  Pallas kernels  28.1 us (91%)
  local copies, waits for them, and re-layouts  1.94 us (6%)
  between operations  0.65 us (2%)
    pallas_call x1, Pallas kernels, on_device(): pl.pallas_call(functools.partial(kernel, rows, cols, COUPLE / math.sqrt(e...  28.1 us
    unnamed x4, local copies, waits for them, and re-layouts  1.94 us

profile of v3, /device:TPU:0, one launch (start us, length us, event | category | flops | bytes accessed | tf_op | source)
XLA Modules:
  0.0 30.7 jit_solution(2903423567849632964)
XLA Ops:
  0.6 28.1 %shard_map.77 = (f32[16,256]{1,0:T(8,128)}, f32[16,256]{1,0:T(8,128)}) custom-call(f32[16,256]{1,0:T(8,128)} %b_hbm.1, f32[1,256]{1,0:T(1,128)} %bitcast.5, f32[2,6400]{1,0:T(2,128)} %xy_hbm.1, f32[2,4096]{1,0:T(2,128)} %offset_hbm.1, s32[32,128]{1,0:T(8,128)} %bitcast.3, s32[32,128]{1,0:T(8,128)} %bitcast.4), custom_call_target="tpu_custom_call" | custom-call | tf_op jit(solution)/shard_map/pallas_call | solution.py:277
  28.7 0.0 copy-start
  28.8 1.3 %copy.10 = f32[16,256]{1,0:T(8,128)} copy(f32[16,256]{1,0:T(8,128)} %get-tuple-element.4) | data formatting | bytes 32768
  30.1 0.0 copy-done
  30.1 0.6 %copy.11 = f32[16,256]{1,0:T(8,128)} copy(f32[16,256]{1,0:T(8,128)S(1)} %copy-done) | data formatting | bytes 32768
Async XLA Ops:
  28.7 1.3 %copy-start = (f32[16,256]{1,0:T(8,128)S(1)}, f32[16,256]{1,0:T(8,128)}, u32[]{:S(2)}) copy-start(f32[16,256]{1,0:T(8,128)} %get-tuple-element.5) | copy-start | bytes 49156

commit v4 on v3

--- a/solution.py
+++ b/solution.py
@@ -49,9 +49,9 @@
 def kernel(
     rows, cols, scale,
     b_hbm, ratio_hbm, xy_hbm, offset_hbm, filament_hbm, order_hbm,
-    solution_ref, residual_ref,
+    out_ref,
     b_ref, ratio_ref, xy_ref, offset_ref, filament_ref, order_ref,
-    offset_tab, xy_tab, near, high_all, low_all, b_all, xy_all, image_all, r_all, dots,
+    offset_tab, xy_tab, near, high_all, low_all, b_all, xy_all, image_all, dots,
     load, send_b, recv_b, send_xy, recv_xy, send_im, recv_im, send_dot, recv_dot,
 ):
     count = rows * cols
@@ -210,35 +210,33 @@
     spread(image_all.at[me], image_all, send_im, recv_im)
     norm = rowsum(squares)
 
+    def add_image(p, carry):
+        turned, products = carry
+        value = image_all[p]
+        return term(p, value, turned), products + b_all[p] * value
+
     def curve(k, carry):
         forward(image_all, send_im, recv_im, k)
-        p = row_at(k) * cols + col
-        return carry + b_all[p] * image_all[p]
+        return add_image(row_at(k) * cols + col, carry)
 
     def curve_other(k, carry):
         p = other(k)
         arrived(image_all, recv_im, p)
-        return carry + b_all[p] * image_all[p]
-
-    carry = lax.fori_loop(1, rows, curve, b * image)
-    curved = rowsum(lax.fori_loop(0, others, curve_other, carry))
-    step = norm / curved
-
-    def reduce_residual(k, carry):
+        return add_image(p, carry)
+
+    carry = fold(1, rows, curve, (term(me, image, zero), b * image))
+    turned, products = fold(0, others, curve_other, carry)
+    step = norm / rowsum(products)
+
+    def residual_squares(k, carry):
         value = b_all[k] - step * image_all[k]
-        r_all[k] = value
         return carry + value * value
 
-    norm_next = rowsum(fold(0, count, reduce_residual, zero))
+    norm_next = rowsum(fold(0, count, residual_squares, zero))
     beta = norm_next / norm
-
-    def second(k, total):
-        return term(k, r_all[k] + beta * b_all[k], total)
-
-    total = fold(0, count, second, zero)
-    residual = r_all[me]
+    residual = b - step * image
     direction = residual + beta * b
-    image2 = diagonal * direction + scale * total
+    image2 = diagonal * direction + scale * ((1.0 + beta) * total - step * turned)
 
     own = (
         lax.broadcasted_iota(jnp.int32, (side, LANES), 0) == lax.broadcasted_iota(jnp.int32, (side, LANES), 1)
@@ -254,8 +252,8 @@
     flat = lax.fori_loop(0, count, lambda k, acc: acc + dots[k], jnp.zeros((1, LANES), jnp.float32))
     curved2 = rowsum(jnp.where(own, flat, 0.0))
     step2 = norm_next / curved2
-    solution_ref[...] = step * b + step2 * direction
-    residual_ref[...] = residual - step2 * image2
+    out_ref[0] = step * b + step2 * direction
+    out_ref[1] = residual - step2 * image2
 
     sent(b_ref, b_all, send_b, recv_b)
     sent(xy_all.at[me], xy_all, send_xy, recv_xy)
@@ -270,15 +268,15 @@
     def on_device(right_side, current_ratio, filament_xy, element_offset, element_filament, element_order):
         side, width = right_side.shape
         elements = width * count
-        shape = jax.ShapeDtypeStruct((side, width), jnp.float32)
+        shape = jax.ShapeDtypeStruct((2, side, width), jnp.float32)
         vmem = pl.BlockSpec(memory_space=pltpu.VMEM)
         f32 = jnp.float32
         blocks = pltpu.VMEM((count, side, width), f32)
-        return pl.pallas_call(
+        out = pl.pallas_call(
             functools.partial(kernel, rows, cols, COUPLE / math.sqrt(elements)),
-            out_shape=(shape, shape),
+            out_shape=shape,
             in_specs=[pl.BlockSpec(memory_space=pltpu.HBM)] * 6,
-            out_specs=(vmem, vmem),
+            out_specs=vmem,
             scratch_shapes=[
                 pltpu.VMEM((side, width), f32),
                 pltpu.VMEM((1, width), f32),
@@ -293,7 +291,6 @@
                 pltpu.VMEM((count, width, width), jnp.bfloat16),
                 blocks,
                 pltpu.VMEM((count, 2, width), f32),
-                blocks,
                 blocks,
                 pltpu.VMEM((count, 1, LANES), f32),
             ]
@@ -311,6 +308,8 @@
             element_order.reshape(elements // LANES, LANES),
         )
 
+        return out[0], out[1]
+
     return jax.shard_map(
         on_device,
         mesh=mesh,

time: 30.9 us -> 29.3 us (0.948)
  Pallas kernels: 28.1 us -> 27 us
  local copies, waits for them, and re-layouts: 1.94 us -> 1.35 us
    unnamed x4 -> x0, local copies, waits for them, and re-layouts: 1.94 us -> none
    squeeze x0 -> x1, local copies, waits for them, and re-layouts: none -> 1.35 us  [on_device(): return (out[0], out[1])]
    pallas_call x1, Pallas kernels: 28.1 us -> 27 us  [on_device(): pl.pallas_call(functools.partial(kernel, rows, cols, COUPLE / math.sqrt(e...]
where the time goes in v4:
time: 29.3 us; the launch traced here: 29 us
  Pallas kernels  27 us (92%)
  local copies, waits for them, and re-layouts  1.35 us (5%)
  between operations  0.64 us (2%)
    pallas_call x1, Pallas kernels, on_device(): pl.pallas_call(functools.partial(kernel, rows, cols, COUPLE / math.sqrt(e...  27 us
    squeeze x1, local copies, waits for them, and re-layouts, on_device(): return (out[0], out[1])  1.35 us

profile of v4, /device:TPU:0, one launch (start us, length us, event | category | flops | bytes accessed | tf_op | source)
XLA Modules:
  0.0 29.0 jit_solution(11462228287427208783)
XLA Ops:
  0.6 27.0 %shard_map.77 = f32[2,16,256]{2,1,0:T(8,128)} custom-call(f32[16,256]{1,0:T(8,128)} %b_hbm.1, f32[1,256]{1,0:T(1,128)} %bitcast.9, f32[2,6400]{1,0:T(2,128)} %xy_hbm.1, f32[2,4096]{1,0:T(2,128)} %offset_hbm.1, s32[32,128]{1,0:T(8,128)} %bitcast.7, s32[32,128]{1,0:T(8,128)} %bitcast.8), custom_call_target="tpu_custom_call" | custom-call | tf_op jit(solution)/shard_map/pallas_call | solution.py:275
  27.6 1.3 %slice_bitcast_fusion = (f32[16,256]{1,0:T(8,128)}, f32[16,256]{1,0:T(8,128)}) fusion(f32[2,16,256]{2,1,0:T(8,128)} %shard_map.77), kind=kLoop, calls=%fused_computation | loop fusion | bytes 65536 | tf_op jit(solution)/shard_map/squeeze | solution.py:311

commit v5 on v4

--- a/solution.py
+++ b/solution.py
@@ -98,8 +98,8 @@
         return push(src, dst_all.at[p], send.at[rows + k * cols + c], recv.at[p], (group, row, col_at(c)))
 
     def spread(src, dst_all, send, recv):
-        loop(rows - 1, lambda k: across(src, dst_all, send, recv, k + 1).start())
         loop(cols - 1, lambda c: beside(src, dst_all, send, recv, 0, c + 1).start())
+        loop(rows - 1, lambda k: across(src, dst_all, send, recv, 1 + (k + rows // 2 - 1) % (rows - 1)).start())
 
     def forward(dst_all, send, recv, k):
         arrived(dst_all, recv, row_at(k) * cols + col)
@@ -199,9 +199,9 @@
         arrived(b_all, recv_b, p)
         return add_first(p, carry)
 
-    lax.fori_loop(1, rows, gather_xy, 0)
+    fold(1, rows, gather_xy, 0)
     couple_other(0, 0)
-    lax.fori_loop(1, rows, lambda k, carry: couple_other(k, gather_b(k, carry)), 0)
+    fold(1, rows, lambda k, carry: couple_other(k, gather_b(k, carry)), 0)
     lax.fori_loop(rows, others, couple_other, 0)
     carry = fold(1, rows, first, (total, b * b))
     total, squares = fold(0, others, first_other, carry)
@@ -247,7 +247,7 @@
     def give(k):
         return push(dots.at[me], dots.at[me], send_dot.at[k], recv_dot.at[me], device(peer(k)))
 
-    loop(count - 1, lambda k: give(k + 1).start())
+    loop(count - 1, lambda k: give(1 + (k + count // 2 - 1) % (count - 1)).start())
     loop(count - 1, lambda k: arrived(dots, recv_dot, peer(k + 1)))
     flat = lax.fori_loop(0, count, lambda k, acc: acc + dots[k], jnp.zeros((1, LANES), jnp.float32))
     curved2 = rowsum(jnp.where(own, flat, 0.0))

time: 29.3 us -> 28.9 us (0.986)
  Pallas kernels: 27 us -> 26.6 us
    pallas_call x1, Pallas kernels: 27 us -> 26.6 us  [on_device(): pl.pallas_call(functools.partial(kernel, rows, cols, COUPLE / math.sqrt(e...]
where the time goes in v5:
time: 28.9 us; the launch traced here: 28.6 us
  Pallas kernels  26.6 us (92%)
  local copies, waits for them, and re-layouts  1.35 us (5%)
  between operations  0.64 us (2%)
    pallas_call x1, Pallas kernels, on_device(): pl.pallas_call(functools.partial(kernel, rows, cols, COUPLE / math.sqrt(e...  26.6 us
    squeeze x1, local copies, waits for them, and re-layouts, on_device(): return (out[0], out[1])  1.35 us

profile of v5, /device:TPU:0, one launch (start us, length us, event | category | flops | bytes accessed | tf_op | source)
XLA Modules:
  0.0 28.6 jit_solution(13822430839423988654)
XLA Ops:
  0.6 26.6 %shard_map.77 = f32[2,16,256]{2,1,0:T(8,128)} custom-call(f32[16,256]{1,0:T(8,128)} %b_hbm.1, f32[1,256]{1,0:T(1,128)} %bitcast.9, f32[2,6400]{1,0:T(2,128)} %xy_hbm.1, f32[2,4096]{1,0:T(2,128)} %offset_hbm.1, s32[32,128]{1,0:T(8,128)} %bitcast.7, s32[32,128]{1,0:T(8,128)} %bitcast.8), custom_call_target="tpu_custom_call" | custom-call | tf_op jit(solution)/shard_map/pallas_call | solution.py:275
  27.2 1.3 %slice_bitcast_fusion = (f32[16,256]{1,0:T(8,128)}, f32[16,256]{1,0:T(8,128)}) fusion(f32[2,16,256]{2,1,0:T(8,128)} %shard_map.77), kind=kLoop, calls=%fused_computation | loop fusion | bytes 65536 | tf_op jit(solution)/shard_map/squeeze | solution.py:311
